TPU v7x, 32 devices: a whole 2x2x4 slice. The times are simulated.
32 devices in a mesh: group: 2 (over y), cable: 8 (over z, x), fold: 2 (over core).
Axes of the slice: x: 2, y: 2, z: 4, core: 2. Of those that a mesh axis runs over, the one named last changes fastest.
Arguments:
- raw: bfloat16 [16, 1024, 1024], P(('group', 'fold'), None, 'cable'), parts along dimension 0, as said below
- seg_count: int32 [32], P('group'), parts along dimension 0, may hold values from 4 to 8
- mask: int32 [2048], P(('group', 'cable')), parts along dimension 0, may hold values 0 or 1
Outputs:
- xcorr: float32 [16, 101, 1024], P(('group', 'fold'), None, 'cable'), parts along dimension 0
There are 2 independent parts, one for each index of `group`. A program takes and returns all parts, laid end to end along the dimension named above; each array names one. Nothing has to cross between parts.
Inputs may be any that keep to these rules, and one draw needn't show every extreme that they name: raw has a scale of its own for each segment and channel.
All inputs are finite; a program needn't handle non-finite values. No bound on the sum of `mask` on one device may be relied on, other than what follows from the above.
Results may differ from a plain program's by a relative error of at most 0.0066.
Values may be sent and summed in bfloat16 or wider, within the bound.
A program may use at most 64 MiB of HBM per device.

v0:
```python
import math

import jax
import jax.numpy as jnp
from jax import lax
from jax.sharding import PartitionSpec as P

CHAN_BLK = 64
LAGS = 101
NOFF = 8


def shifted(shard, axis, by):
    size = lax.axis_size(axis)
    pairs = [(i, i + by) for i in range(size) if 0 <= i + by < size]
    return lax.ppermute(shard, axis, pairs)


def forward_table(samples, bins):
    times = jnp.arange(samples, dtype=jnp.int32)
    freqs = jnp.arange(bins, dtype=jnp.int32)
    phase = (times[:, None] * freqs[None, :] % samples).astype(jnp.float32) * (
        2.0 * math.pi / samples
    )
    return jnp.concatenate([jnp.cos(phase), -jnp.sin(phase)], axis=1).astype(jnp.bfloat16)


def lag_table(samples, bins, lags):
    freqs = jnp.arange(bins, dtype=jnp.int32)
    offsets = jnp.arange(lags, dtype=jnp.int32) - lags // 2 + samples
    phase = (freqs[:, None] * offsets[None, :] % samples).astype(jnp.float32) * (
        2.0 * math.pi / samples
    )
    return jnp.concatenate([jnp.cos(phase), -jnp.sin(phase)], axis=0) / math.sqrt(bins)


def normalize(record, axis):
    values = record.astype(jnp.float32)
    spread = jnp.sqrt(jnp.mean(values * values, axis=axis, keepdims=True) + 1e-06)
    return (jnp.clip(values, -2.0 * spread, 2.0 * spread) / spread).astype(jnp.bfloat16)


def whiten(spectrum, usable, bins):
    real_part = spectrum[..., :bins, :]
    imag_part = spectrum[..., bins:, :]
    power = real_part * real_part + imag_part * imag_part
    widths = ((0, 0),) * (power.ndim - 2) + ((2, 2), (0, 0))
    padded = jnp.pad(power, widths)
    smooth = (
        padded[..., 0:bins, :]
        + padded[..., 1 : bins + 1, :]
        + padded[..., 2 : bins + 2, :]
        + padded[..., 3 : bins + 3, :]
        + padded[..., 4 : bins + 4, :]
    ) / 5.0
    level = smooth + 0.01 * jnp.mean(power, axis=-2, keepdims=True)
    factor = usable / jnp.sqrt(level)
    return jnp.concatenate([real_part * factor, imag_part * factor], axis=-2).astype(jnp.bfloat16)


def cross(first, second, bins):
    left = first.astype(jnp.float32)
    right = second.astype(jnp.float32)
    left_re, left_im = (left[..., :bins, :], left[..., bins:, :])
    right_re, right_im = (right[..., :bins, :], right[..., bins:, :])
    return jnp.concatenate(
        [left_re * right_re + left_im * right_im, left_im * right_re - left_re * right_im], axis=-2
    )


def body(raw, seg_count, mask):
    seg_dev, samples, chan_local = raw.shape
    bins = samples // 2
    blocks_here = chan_local // CHAN_BLK
    reach = NOFF * CHAN_BLK // chan_local
    fold_at = lax.axis_index("fold")
    cable_at = lax.axis_index("cable")
    clipped = normalize(raw, 1)
    spectrum = jnp.einsum(
        "tg,stc->sgc", forward_table(samples, bins), clipped, preferred_element_type=jnp.float32
    )
    white = whiten(spectrum, mask.astype(jnp.float32)[None, None, :], bins)
    pieces = [white]
    for step in range(1, reach + 1):
        pieces.append(shifted(white, "cable", -step))
    extended = jnp.concatenate(pieces, axis=2)
    padded_blocks = jnp.concatenate([seg_count, jnp.zeros((reach * blocks_here,), jnp.int32)])
    window = lax.dynamic_slice_in_dim(
        padded_blocks, cable_at * blocks_here, blocks_here * (1 + reach), 0
    )
    chan_count = (window[:, None] * jnp.ones((1, CHAN_BLK), jnp.int32)).reshape(-1)
    seg_index = fold_at * seg_dev + jnp.arange(seg_dev, dtype=jnp.int32)
    terms = []
    for k in range(1, NOFF + 1):
        other = lax.slice_in_dim(extended, k * CHAN_BLK, k * CHAN_BLK + chan_local, axis=2)
        pair_count = jnp.minimum(
            chan_count[:chan_local], chan_count[k * CHAN_BLK : k * CHAN_BLK + chan_local]
        )
        divisor = jnp.maximum(pair_count, 1).astype(jnp.float32)
        weight = (seg_index[:, None] < pair_count[None, :]).astype(jnp.float32)
        summed = jnp.sum(cross(white, other, bins) * weight[:, None, :], axis=0)
        terms.append(summed / divisor[None, :])
    stack = jnp.stack(terms)
    inverse = lag_table(samples, bins, LAGS)
    own = lax.psum_scatter(stack, "fold", scatter_dimension=0, tiled=True)
    return jnp.einsum("kgc,gl->klc", own, inverse, precision=lax.Precision.HIGHEST)


def solution(mesh):
    in_specs = (P(("group", "fold"), None, "cable"), P("group"), P(("group", "cable")))
    out_specs = P(("group", "fold"), None, "cable")
    return jax.shard_map(body, mesh=mesh, in_specs=in_specs, out_specs=out_specs, check_vma=False)
```

profile of v0, /device:TPU:1, one launch (start us, length us, event | category | flops | bytes accessed | tf_op | source)
XLA Modules:
  0.0 199.7 jit_solution(15542960966018196127)
XLA Ops:
  6.5 8.5 %negate_convert_fusion = (bf16[1024,512]{1,0:T(8,128)(2,1)S(1)}, bf16[1024,512]{1,0:T(8,128)(2,1)S(1)}) fusion(), kind=kLoop, calls=%fused_computation.32 | loop fusion | flops 8912896 | bytes 2097152 | tf_op jit(solution)/shard_map/convert.3
  15.1 0.2 fusion
  15.3 1.3 fusion.21
  16.6 0.2 fusion.63
  16.9 0.4 copy-done.1
  17.3 1.2 multiply_convert_fusion.1
  18.6 0.3 multiply_convert_fusion
  18.8 1.1 pad_maximum_fusion.5
  20.0 1.3 collective-permute-start
  21.3 1.3 collective-permute-start.1
  22.6 1.3 collective-permute-start.2
  23.9 1.5 collective-permute-start.3
  25.6 0.1 min.127
  25.7 0.1 min.129
  25.9 0.1 min.131
  26.0 0.1 min.133
  26.2 0.1 min.135
  26.4 0.1 min.137
  26.5 0.1 min.139
  26.9 20.1 %collective-permute-done = bf16[4,1024,128]{1,2,0:T(8,128)(2,1)S(1)} collective-permute-done((bf16[4,1024,128]{1,2,0:T(8,128)(2,1)}, bf16[4,1024,128]{1,2,0:T(8,128)(2,1)S(1)}, u32[]{:S(2)}, u32[]{:S(2)}) %collective-permute-start) | collective-permute-done | bytes 1048608 | tf_op jit(solution)/shard_map/ppermute | solution.py:16
  47.0 23.4 %collective-permute-done.1 = bf16[4,1024,128]{1,2,0:T(8,128)(2,1)S(1)} collective-permute-done((bf16[4,1024,128]{1,2,0:T(8,128)(2,1)}, bf16[4,1024,128]{1,2,0:T(8,128)(2,1)S(1)}, u32[]{:S(2)}, u32[]{:S(2)}) %collective-permute-start.1) | collective-permute-done | bytes 1048608 | tf_op jit(solution)/shard_map/ppermute | solution.py:16
  70.4 2.0 %collective-permute-done.2 = bf16[4,1024,128]{1,2,0:T(8,128)(2,1)} collective-permute-done((bf16[4,1024,128]{1,2,0:T(8,128)(2,1)}, bf16[4,1024,128]{1,2,0:T(8,128)(2,1)}, u32[]{:S(2)}, u32[]{:S(2)}) %collective-permute-start.2) | collective-permute-done | bytes 1048608 | tf_op jit(solution)/shard_map/ppermute | solution.py:16
  72.4 88.9 %collective-permute-done.3 = bf16[4,1024,128]{1,2,0:T(8,128)(2,1)} collective-permute-done((bf16[4,1024,128]{1,2,0:T(8,128)(2,1)}, bf16[4,1024,128]{1,2,0:T(8,128)(2,1)}, u32[]{:S(2)}, u32[]{:S(2)}) %collective-permute-start.3) | collective-permute-done | bytes 1048608 | tf_op jit(solution)/shard_map/ppermute | solution.py:16
  161.3 3.9 %fusion.64 = (f32[4,1024,128]{1,2,0:T(8,128)S(1)}, f32[4,1024,128]{1,2,0:T(8,128)S(1)}, f32[4,1024,128]{1,2,0:T(8,128)S(1)}, f32[4,1024,128]{1,2,0:T(8,128)S(1)}...) fusion(bf16[4,1024,128]{1,2,0:T(8,128)(2,1)} %collective-permut, ...), kind=kLoop, calls=%fused_computation.151 | loop fusion | flops 13631488 | bytes 24117248 | tf_op jit(solution)/shard_map/convert_element_type | solution.py:63
  165.2 0.8 multiply_add_fusion
  166.0 0.8 multiply_add_fusion.1
  166.8 0.8 multiply_add_fusion.2
  167.6 0.9 multiply_add_fusion.3
  168.4 0.2 fusion.10
  168.7 0.9 fusion.45
  169.6 0.2 fusion.17
  169.8 0.2 fusion.16
  170.0 0.2 fusion.15
  170.2 0.2 fusion.14
  170.4 0.2 fusion.13
  170.7 0.2 fusion.12
  170.9 0.2 fusion.11
  171.1 0.9 fusion.44
  172.0 0.9 fusion.43
  172.9 0.9 fusion.42
  173.9 0.9 fusion.41
  174.8 0.9 fusion.40
  175.7 0.9 fusion.39
  176.6 0.9 fusion.38
  177.5 0.9 fusion.57
  178.5 9.9 %reduce-scatter.2.cloned.1.call-done = f32[4,1024,128]{1,2,0:T(8,128)} async-done(((f32[8,1024,128]{1,2,0:T(8,128)}), f32[4,1024,128]{1,2,0:T(8,128)}) %reduce-scatter.2.cloned.1.call-update) | async-done | bytes 2097168 | tf_op jit(solution)/shard_map/reduce_scatter | solution.py:105
  188.4 3.7 %convolution_bitcast_fusion = f32[4,101,128]{2,1,0:T(8,128)S(1)} fusion(f32[4,1024,128]{1,2,0:T(8,128)} %reduce-scatter.2.cloned.1.call-done, f32[512,101]{0,1:T(8,128)S(1)} %get-tuple-element.46, f32[512,101]{0,1:T(8,128)S(1)} %get-tuple-element.45), kind=kOutput, calls=%fused_computation.42 | convolution fusion | flops 635643904 | bytes 2717696 | tf_op jit(solution)/shard_map/kgc,gl->klc/dot_general | solution.py:106
  192.1 0.7 copy.8
  (32 shorter events, 1.0 us)
Async XLA Ops:
  6.5 8.6 %copy-start = (bf16[4,1024,128]{2,1,0:T(8,128)(2,1)S(1)}, bf16[4,1024,128]{2,1,0:T(8,128)(2,1)}, u32[]{:S(2)}) copy-start(bf16[4,1024,128]{2,1,0:T(8,128)(2,1)} %param.3) | copy-start | bytes 3145732
  6.5 181.9 %reduce-scatter.2.cloned.1.call-start = ((), (), s32[]{:S(2)}) async-start(), calls=%async_computation.1 | async-start | bytes 6291456 | tf_op jit(solution)/shard_map/reduce_scatter | solution.py:105
  16.6 0.7 copy-start.1
  18.5 6.8 %copy-start.2 = (s32[16]{0:T(128)S(1)}, s32[16]{0:T(128)}, u32[]{:S(2)}) copy-start(s32[16]{0:T(128)} %param.4) | copy-start | bytes 196
  20.0 27.0 %collective-permute-start = (bf16[4,1024,128]{1,2,0:T(8,128)(2,1)}, bf16[4,1024,128]{1,2,0:T(8,128)(2,1)S(1)}, u32[]{:S(2)}, u32[]{:S(2)}) collective-permute-start(bf16[4,1024,128]{1,2,0:T(8,128)(2,1)} %pad_maximum_fusion.5), channel_id=1, source_target_pairs={{2,0},{4,2},{6,4},{8,6},{10,8},{12,10},{14,12},{3,1},{5,3},{7,5},{... | collective-permute-start | bytes 3145736 | tf_op jit(solution)/shard_map/ppermute | solution.py:16
  21.3 49.2 %collective-permute-start.1 = (bf16[4,1024,128]{1,2,0:T(8,128)(2,1)}, bf16[4,1024,128]{1,2,0:T(8,128)(2,1)S(1)}, u32[]{:S(2)}, u32[]{:S(2)}) collective-permute-start(bf16[4,1024,128]{1,2,0:T(8,128)(2,1)} %pad_maximum_fusion.5), channel_id=1, source_target_pairs={{4,0},{6,2},{8,4},{10,6},{12,8},{14,10},{5,1},{7,3},{9,5},{11,7},{... | collective-permute-start | bytes 3145736 | tf_op jit(solution)/shard_map/ppermute | solution.py:16
  22.6 49.9 %collective-permute-start.2 = (bf16[4,1024,128]{1,2,0:T(8,128)(2,1)}, bf16[4,1024,128]{1,2,0:T(8,128)(2,1)}, u32[]{:S(2)}, u32[]{:S(2)}) collective-permute-start(bf16[4,1024,128]{1,2,0:T(8,128)(2,1)} %pad_maximum_fusion.5), channel_id=1, source_target_pairs={{6,0},{8,2},{10,4},{12,6},{14,8},{7,1},{9,3},{11,5},{13,7},{15,9},... | collective-permute-start | bytes 3145736 | tf_op jit(solution)/shard_map/ppermute | solution.py:16
  23.9 137.5 %collective-permute-start.3 = (bf16[4,1024,128]{1,2,0:T(8,128)(2,1)}, bf16[4,1024,128]{1,2,0:T(8,128)(2,1)}, u32[]{:S(2)}, u32[]{:S(2)}) collective-permute-start(bf16[4,1024,128]{1,2,0:T(8,128)(2,1)} %pad_maximum_fusion.5), channel_id=1, source_target_pairs={{8,0},{10,2},{12,4},{14,6},{9,1},{11,3},{13,5},{15,7},{24,16},{26,... | collective-permute-start | bytes 3145736 | tf_op jit(solution)/shard_map/ppermute | solution.py:16
Sparse Core Ops, SparseCore 0:
  177.7 10.6 reduce-scatter.1
where the time goes:
time: 200 us
  waiting for transfers between devices  144 us (72%)
  other arithmetic  28.8 us (14%)
  between operations  13.7 us (7%)
  starting transfers between devices  5.34 us (3%)
  matrix products  5.01 us (3%)
  local copies, waits for them, and re-layouts  2.48 us (1%)
    ppermute x4, waiting for transfers between devices, shifted(): return lax.ppermute(shard, axis, pairs)  134 us
    another operation x3, other arithmetic  10 us
    reduce_scatter x1, waiting for transfers between devices, body(): own = lax.psum_scatter(stack, 'fold', scatter_dimension=0, tiled=True)  9.92 us
    unnamed x7, other arithmetic  6.39 us
    ppermute x4, starting transfers between devices, shifted(): return lax.ppermute(shard, axis, pairs)  5.34 us
  transfers between devices with their start and end apart: 5, of which 5 were waited for; matrix products, arithmetic and copies ran while one was open for 1% of the time, Pallas kernels for 0%

commit v1 on v0

v1 whole, which is shorter than its diff:
```python
import functools
import math

import jax
import jax.numpy as jnp
import ml_dtypes
import numpy as np
from jax import lax
from jax.experimental import pallas as pl
from jax.experimental.pallas import tpu as pltpu
from jax.sharding import PartitionSpec as P

CHAN_BLK = 64
LAGS = 101
ROWS = 112
NOFF = 8
HALF = NOFF // 2
F32 = jnp.float32
BF16 = jnp.bfloat16
MESH = pl.DeviceIdType.MESH


def forward_table(samples):
    bins = samples // 2
    phase = np.outer(np.arange(bins), np.arange(samples)) % samples * (2.0 * math.pi / samples)
    return np.concatenate([np.cos(phase), -np.sin(phase)], axis=0).astype(ml_dtypes.bfloat16)


def lag_table(samples):
    bins = samples // 2
    lag = np.arange(LAGS) - LAGS // 2 + samples
    phase = np.outer(lag, np.arange(bins)) % samples * (2.0 * math.pi / samples)
    table = np.concatenate([np.cos(phase), -np.sin(phase)], axis=1) / math.sqrt(bins)
    full = np.zeros((ROWS, samples), np.float64)
    full[:LAGS] = table
    return full.astype(ml_dtypes.bfloat16)


MID = [(0, 7), (0, 8), (1, 5), (1, 6), (1, 7), (1, 8)]
HOME = [(0, 5), (0, 6), (0, 7), (1, 5), (0, 1), (0, 2), (0, 3), (0, 4), (1, 1), (1, 2), (1, 3), (1, 4)]


def kernel(
    size,
    raw, mask, cnt, basis_hbm, inv,
    out,
    basis, own_raw, nb_raw, mask_out, mask_in, spec, power, w0, wu, wl, prods, acc,
    home, mid, home_in, mid_in, hsend, msend, hrecv, mrecv,
    load_sem, xs, xr, us, ur, ds, dr, cs, cr, es, er, ms, mr,
):
    samples = raw.shape[1]
    bins = samples // 2
    cable = lax.axis_index("cable")
    fold = lax.axis_index("fold")
    side = cable % 2
    node = cable // 2
    has_up = node < size // 2 - 1
    has_dn = node > 0
    peer = cable + 1 - 2 * side
    nblk = cnt.shape[0]
    seg_dev = raw.shape[0]
    kept = seg_dev // 2

    def remote(src, dst, ssem, rsem, at, core):
        return pltpu.make_async_remote_copy(
            src_ref=src, dst_ref=dst, send_sem=ssem, recv_sem=rsem,
            device_id={"cable": at, "fold": core}, device_id_type=MESH,
        )

    raw_load = [
        pltpu.make_async_copy(raw.at[kept * side + s], own_raw.at[s], load_sem.at[s])
        for s in range(kept)
    ]
    basis_load = pltpu.make_async_copy(basis_hbm, basis, load_sem.at[kept])
    raw_load[0].start()
    basis_load.start()
    for s in range(1, kept):
        raw_load[s].start()
    mask_out[...] = jnp.broadcast_to(mask[...], mask_out.shape)

    barrier = pltpu.get_barrier_semaphore()

    def greet(at, core):
        pl.semaphore_signal(barrier, inc=1, device_id={"cable": at, "fold": core}, device_id_type=MESH)

    greet(peer, fold)
    greet(cable, 1 - fold)

    @pl.when(has_up)
    def _():
        greet(cable + 2, fold)
        greet(peer + 2, fold)

    @pl.when(has_dn)
    def _():
        greet(cable - 2, fold)
        greet(peer - 2, fold)

    peers = 2 + jnp.where(has_up, 2, 0) + jnp.where(has_dn, 2, 0)
    pl.semaphore_wait(barrier, peers)

    x_raw = [
        remote(raw.at[kept * (1 - side) + s], nb_raw.at[s], xs.at[s], xr.at[s], peer, fold)
        for s in range(kept)
    ]
    x_mask = remote(mask_out, mask_in, xs.at[kept], xr.at[kept], peer, fold)
    x_mask.start()
    for copy in x_raw:
        copy.start()

    power[0:8, :] = jnp.zeros((8, 128), F32)
    power[bins + 8 : bins + 16, :] = jnp.zeros((8, 128), F32)
    zero_tile = jnp.zeros((ROWS, 128), BF16)
    home[1, 0, 3] = zero_tile
    for kk in range(1, 4):
        home[1, 1, kk] = zero_tile
    mid[0, 0] = zero_tile
    mid[0, 1] = zero_tile

    @pl.when(jnp.logical_not(has_up))
    def _():
        @pl.loop(0, bins * 2 // 64)
        def _(t):
            at = pl.ds(pl.multiple_of(t * 64, 64), 64)
            for s in range(kept):
                for col in range(2):
                    wu[s, col, at, :] = jnp.zeros((64, 128), BF16)

    @pl.when(jnp.logical_not(has_dn))
    def _():
        @pl.loop(0, bins * 2 // 64)
        def _(t):
            at = pl.ds(pl.multiple_of(t * 64, 64), 64)
            for s in range(kept):
                for col in range(2):
                    wl[s, col, at, :] = jnp.zeros((64, 128), BF16)

    lane = lax.broadcasted_iota(jnp.int32, (1, 128), 1)
    low = lane < CHAN_BLK

    def whiten(source, usable, owner, s, dst):
        seg = fold * seg_dev + kept * side + s
        count = jnp.where(low, cnt[2 * owner], cnt[2 * owner + 1])
        keep = jnp.where(seg < count, usable.astype(F32), 0.0)

        def squares(t, total):
            v = source[pl.ds(pl.multiple_of(t * 64, 64), 64), :].astype(F32)
            return total + jnp.sum((v * v).reshape(8, 8, 128), axis=0)

        total = lax.fori_loop(0, samples // 64, squares, jnp.zeros((8, 128), F32))
        mean = jnp.sum(total, axis=0, keepdims=True) * (1.0 / samples)
        rate = lax.rsqrt(mean + 1e-06)
        clipped = jnp.clip(source[...].astype(F32) * rate, -2.0, 2.0).astype(BF16)

        @pl.loop(0, samples // 256)
        def _(t):
            at = pl.ds(pl.multiple_of(t * 256, 256), 256)
            spec[at, :] = jnp.dot(basis[at, :], clipped, preferred_element_type=F32)

        def powers(t, total):
            at = pl.multiple_of(t * 64, 64)
            re = spec[pl.ds(at, 64), :]
            im = spec[pl.ds(bins + at, 64), :]
            p = re * re + im * im
            power[pl.ds(8 + at, 64), :] = p
            return total + jnp.sum(p.reshape(8, 8, 128), axis=0)

        total = lax.fori_loop(0, bins // 64, powers, jnp.zeros((8, 128), F32))
        floor = jnp.sum(total, axis=0, keepdims=True) * (0.01 / bins)

        @pl.loop(0, bins // 64)
        def _(t):
            at = pl.multiple_of(t * 64, 64)
            wide = power[pl.ds(at, 80), :]
            smooth = wide[6:70] + wide[7:71] + wide[8:72] + wide[9:73] + wide[10:74]
            factor = keep * lax.rsqrt(smooth * 0.2 + floor)
            dst[pl.ds(at, 64), :] = (spec[pl.ds(at, 64), :] * factor).astype(BF16)
            dst[pl.ds(bins + at, 64), :] = (spec[pl.ds(bins + at, 64), :] * factor).astype(BF16)

    def chunk_copies(q, s, col):
        up = remote(w0.at[s, col], wl.at[s, col], us.at[q], dr.at[q], cable + 2, fold)
        dn = remote(w0.at[s, col], wu.at[s, col], ds.at[q], ur.at[q], cable - 2, fold)
        return up, dn

    def send(q, s, col):
        up, dn = chunk_copies(q, s, col)

        @pl.when(has_up)
        def _():
            up.start()

        @pl.when(has_dn)
        def _():
            dn.start()

    def arrive(q, s, col):
        up, dn = chunk_copies(q, s, col)

        @pl.when(has_dn)
        def _():
            up.wait_recv()

        @pl.when(has_up)
        def _():
            dn.wait_recv()

    def crosses(s):
        @pl.loop(0, bins // 16)
        def _(t):
            at = pl.multiple_of(t * 16, 16)

            def load(ref, col):
                return (
                    ref[s, col, pl.ds(at, 16), :].astype(F32),
                    ref[s, col, pl.ds(bins + at, 16), :].astype(F32),
                )

            e0, e1 = load(w0, 0), load(w0, 1)
            u0, u1 = load(wu, 0), load(wu, 1)
            l0, l1 = load(wl, 0), load(wl, 1)
            swap = lambda pair: tuple(pltpu.roll(v, CHAN_BLK, 1) for v in pair)
            join = lambda a, b: tuple(jnp.where(low, p, q) for p, q in zip(a, b))
            zero = (jnp.zeros((16, 128), F32),) * 2
            re0, re1, ru0, ru1 = swap(e0), swap(e1), swap(u0), swap(u1)
            o0, o1, o2, o3 = join(re0, re1), join(re1, ru0), join(ru0, ru1), join(ru1, zero)
            v0 = join(zero, ru0)
            ext = {(0, 1): o0, (0, 2): e1, (0, 3): o1, (0, 4): u0, (0, 5): o2, (0, 6): u1, (0, 7): o3,
                   (1, 1): o1, (1, 2): u0, (1, 3): o2, (1, 4): u1, (1, 5): o3}
            far = {(0, 7): v0, (0, 8): u0, (1, 5): v0, (1, 6): u0, (1, 7): o2, (1, 8): u1}
            jobs = [((l0, l1)[key[0]], far[key]) for key in MID]
            jobs += [((e0, e1)[key[0]], ext[key]) for key in HOME]
            for i, (a, b) in enumerate(jobs):
                lanes = slice(i % 2 * 128, i % 2 * 128 + 128)
                prods[i // 2, pl.ds(at, 16), lanes] = (a[0] * b[0] + a[1] * b[1]).astype(BF16)
                prods[i // 2, pl.ds(bins + at, 16), lanes] = (a[1] * b[0] - a[0] * b[1]).astype(BF16)

    def slot(i):
        if i < len(MID):
            col, k = MID[i]
            return mid.at[col, k - 1 - HALF]
        col, k = HOME[i - len(MID)]
        return home.at[(k - 1) // HALF, col, (k - 1) % HALF]

    def lags(i):
        return jnp.dot(inv[...], prods[i], preferred_element_type=F32)

    own_at, nb_at = side, 1 - side
    raw_load[0].wait()
    basis_load.wait()
    whiten(own_raw.at[0], mask[...], cable, 0, w0.at[0, own_at])
    send(0, 0, own_at)
    raw_load[1].wait()
    whiten(own_raw.at[1], mask[...], cable, 1, w0.at[1, own_at])
    x_mask.wait_recv()
    x_raw[0].wait_recv()
    whiten(nb_raw.at[0], mask_in[0:1, :], peer, 0, w0.at[0, nb_at])
    send(1, 0, nb_at)
    send(2, 1, own_at)
    x_raw[1].wait_recv()
    whiten(nb_raw.at[1], mask_in[0:1, :], peer, 1, w0.at[1, nb_at])
    send(3, 1, nb_at)

    arrive(0, 0, own_at)
    arrive(1, 0, nb_at)
    crosses(0)
    for i in range(9):
        acc[i] = lags(i)
    arrive(2, 1, own_at)
    arrive(3, 1, nb_at)
    crosses(1)

    def finish(i):
        total = acc[i] + lags(i)
        slot(2 * i)[...] = total[:, :128].astype(BF16)
        slot(2 * i + 1)[...] = total[:, 128:].astype(BF16)

    for i in range(3):
        finish(i)
    c_mid = remote(mid, mid_in, cs.at[0], cr.at[0], cable, 1 - fold)

    @pl.when(fold == 0)
    def _():
        c_mid.start()

    for i in range(3, 9):
        finish(i)
    c_home = remote(home.at[1 - fold], home_in, cs.at[1], cr.at[1], cable, 1 - fold)
    c_home.start()

    m_near = remote(msend.at[side], mrecv.at[0], ms.at[0], mr.at[0], cable - 2, fold)
    m_diag = remote(msend.at[1 - side], mrecv.at[1], ms.at[1], mr.at[1], peer - 2, fold)

    @pl.when(fold == 1)
    def _():
        c_mid.wait_recv()
        for col in range(2):
            for kk in range(HALF):
                msend[col, kk] = (mid[col, kk].astype(F32) + mid_in[col, kk].astype(F32)).astype(BF16)

        @pl.when(has_dn)
        def _():
            m_near.start()
            m_diag.start()

    c_home.wait_recv()
    for kk in range(HALF):
        hsend[kk] = (
            home[fold, 1 - side, kk].astype(F32) + home_in[1 - side, kk].astype(F32)
        ).astype(BF16)
    e_home = remote(hsend, hrecv, es.at[0], er.at[0], peer, fold)
    e_home.start()
    for kk in range(HALF):
        acc[0, :, 0:128] = home[fold, side, kk].astype(F32) + home_in[side, kk].astype(F32)
        out[kk] = acc[0, 0:LAGS, 0:128]
    e_home.wait_recv()

    def count_of(block):
        return jnp.where(block < nblk, cnt[jnp.minimum(block, nblk - 1)], 0)

    with_mid = jnp.logical_and(fold == 1, has_up)

    @pl.when(with_mid)
    def _():
        m_near.wait_recv()
        m_diag.wait_recv()
        for kk in range(HALF):
            acc[0, :, 0:128] = mrecv[0, kk].astype(F32) + mrecv[1, kk].astype(F32)
            out[kk] += acc[0, 0:LAGS, 0:128]

    for kk in range(HALF):
        k = fold * HALF + kk + 1
        pair = [jnp.minimum(cnt[2 * cable + b], count_of(2 * cable + b + k)) for b in range(2)]
        divisor = jnp.maximum(jnp.where(low, pair[0], pair[1]), 1).astype(F32)
        acc[0, :, 0:128] = hrecv[kk].astype(F32)
        out[kk] = (out[kk] + acc[0, 0:LAGS, 0:128]) / divisor

    x_mask.wait_send()
    for copy in x_raw:
        copy.wait_send()
    for q, (s, col) in enumerate([(0, own_at), (0, nb_at), (1, own_at), (1, nb_at)]):
        up, dn = chunk_copies(q, s, col)

        @pl.when(has_up)
        def _():
            up.wait_send()

        @pl.when(has_dn)
        def _():
            dn.wait_send()

    @pl.when(fold == 0)
    def _():
        c_mid.wait_send()

    c_home.wait_send()
    e_home.wait_send()

    @pl.when(jnp.logical_and(fold == 1, has_dn))
    def _():
        m_near.wait_send()
        m_diag.wait_send()


def body(size, raw, seg_count, mask):
    seg_dev, samples, chan = raw.shape
    kept = seg_dev // 2
    vmem = pl.BlockSpec(memory_space=pltpu.VMEM)
    dma = pltpu.SemaphoreType.DMA
    white = pltpu.VMEM((kept, 2, samples, 128), BF16)
    lagged = pltpu.VMEM((2, HALF, ROWS, 128), BF16)
    return pl.pallas_call(
        functools.partial(kernel, size),
        out_shape=jax.ShapeDtypeStruct((HALF, LAGS, chan), F32),
        in_specs=[
            pl.BlockSpec(memory_space=pl.ANY),
            vmem,
            pl.BlockSpec(memory_space=pltpu.SMEM),
            pl.BlockSpec(memory_space=pl.ANY),
            vmem,
        ],
        out_specs=vmem,
        scratch_shapes=[
            pltpu.VMEM((samples, samples), BF16),
            pltpu.VMEM((kept, samples, 128), BF16),
            pltpu.VMEM((kept, samples, 128), BF16),
            pltpu.VMEM((8, 128), jnp.int32),
            pltpu.VMEM((8, 128), jnp.int32),
            pltpu.VMEM((samples, 128), F32),
            pltpu.VMEM((samples // 2 + 16, 128), F32),
            white, white, white,
            pltpu.VMEM((9, samples, 256), BF16),
            pltpu.VMEM((9, ROWS, 256), F32),
            pltpu.VMEM((2, 2, HALF, ROWS, 128), BF16),
            lagged,
            lagged,
            lagged,
            pltpu.VMEM((HALF, ROWS, 128), BF16),
            lagged,
            pltpu.VMEM((HALF, ROWS, 128), BF16),
            lagged,
            dma((kept + 1,)),
            dma((kept + 1,)), dma((kept + 1,)),
            dma((4,)), dma((4,)), dma((4,)), dma((4,)),
            dma((2,)), dma((2,)),
            dma((1,)), dma((1,)),
            dma((2,)), dma((2,)),
        ],
        compiler_params=pltpu.CompilerParams(
            collective_id=0, has_side_effects=True, vmem_limit_bytes=40 * 1024 * 1024
        ),
        cost_estimate=pl.CostEstimate(flops=3 * 10**9, bytes_accessed=8 * 10**6, transcendentals=0),
    )(raw, mask.reshape(1, chan), seg_count, jnp.asarray(forward_table(samples)), jnp.asarray(lag_table(samples)))


def solution(mesh):
    in_specs = (P(("group", "fold"), None, "cable"), P("group"), P(("group", "cable")))
    out_specs = P(("group", "fold"), None, "cable")
    run = functools.partial(body, mesh.shape["cable"])
    return jax.shard_map(run, mesh=mesh, in_specs=in_specs, out_specs=out_specs, check_vma=False)
```

time: 200 us -> 48.6 us (0.24)
  waiting for transfers between devices: 144 us -> 0 us
  Pallas kernels: 0 us -> 42.6 us
  other arithmetic: 28.8 us -> 0 us
  between operations: 13.7 us -> 0.01 us
  starting transfers between devices: 5.34 us -> 0 us
  matrix products: 5.01 us -> 0 us
  local copies, waits for them, and re-layouts: 2.48 us -> 5.8 us
    ppermute x4 -> x0, waiting for transfers between devices: 134 us -> none  [shifted(): return lax.ppermute(shard, axis, pairs)]
    pallas_call x0 -> x1, Pallas kernels: none -> 42.6 us  [body(): pl.pallas_call(functools.partial(kernel, size), out_shape=jax.ShapeDtypeS...]
    another operation x4 -> x0, other arithmetic: 11 us -> none
    reduce_scatter x1 -> x0, waiting for transfers between devices: 9.92 us -> none  [body(): own = lax.psum_scatter(stack, 'fold', scatter_dimension=0, tiled=True)]
    unnamed x7 -> x0, other arithmetic: 6.39 us -> none
    ppermute x4 -> x0, starting transfers between devices: 5.34 us -> none  [shifted(): return lax.ppermute(shard, axis, pairs)]
    dot_general x2 -> x0, matrix products: 5.01 us -> none  [the longest x1 3.71 us: body(): jnp.einsum('kgc,gl->klc', own, inverse, precision=lax.Precision.HIGHEST)]
    unnamed x6 -> x10, local copies, waits for them, and re-layouts: 0.43 us -> 5.06 us
  transfers between devices with their start and end apart: 5 -> 0, of which waited for: 5 -> 0; matrix products, arithmetic and copies ran while one was open for 1% -> 0% of each run, Pallas kernels for 0% -> 0%
where the time goes in v1:
time: 48.6 us; the launch traced here: 48.4 us
  Pallas kernels  42.6 us (88%)
  local copies, waits for them, and re-layouts  5.8 us (12%)
    pallas_call x1, Pallas kernels, body(): pl.pallas_call(functools.partial(kernel, size), out_shape=jax.ShapeDtypeS...  42.6 us
    unnamed x10, local copies, waits for them, and re-layouts  5.06 us

profile of v1, /device:TPU:1, one launch (start us, length us, event | category | flops | bytes accessed | tf_op | source)
XLA Modules:
  0.0 48.4 jit_solution(14775470926894313662)
XLA Ops:
  0.0 0.0 copy-start
  0.0 1.2 %copy-done = bf16[4,1024,128]{2,1,0:T(8,128)(2,1)S(1)} copy-done((bf16[4,1024,128]{2,1,0:T(8,128)(2,1)S(1)}, bf16[4,1024,128]{2,1,0:T(8,128)(2,1)}, u32[]{:S(2)}) %copy-start) | copy-done | bytes 1048600
  1.2 0.0 copy-start.1
  1.2 0.7 %copy-done.1 = s32[128]{0:T(128)S(1)} copy-done((s32[128]{0:T(128)S(1)}, s32[128]{0:T(128)}, u32[]{:S(2)}) %copy-start.1) | copy-done | bytes 536
  1.9 0.0 copy-start.2
  1.9 0.7 %copy-done.2 = s32[16]{0:T(128)S(1)} copy-done((s32[16]{0:T(128)S(1)}, s32[16]{0:T(128)}, u32[]{:S(2)}) %copy-start.2) | copy-done | bytes 88
  2.5 0.0 copy-start.3
  2.5 1.6 %copy-done.3 = bf16[1024,1024]{1,0:T(8,128)(2,1)S(1)} copy-done((bf16[1024,1024]{1,0:T(8,128)(2,1)S(1)}, bf16[1024,1024]{1,0:T(8,128)(2,1)}, u32[]{:S(2)}) %copy-start.3) | copy-done | bytes 2097176
  4.1 0.0 copy-start.4
  4.1 0.9 %copy-done.4 = bf16[112,1024]{1,0:T(8,128)(2,1)S(1)} copy-done((bf16[112,1024]{1,0:T(8,128)(2,1)S(1)}, bf16[112,1024]{1,0:T(8,128)(2,1)}, u32[]{:S(2)}) %copy-start.4) | copy-done | bytes 229400
  5.1 42.6 %shard_map.55 = f32[4,101,128]{2,1,0:T(8,128)S(1)} custom-call(bf16[4,1024,128]{2,1,0:T(8,128)(2,1)S(1)} %copy-done, s32[1,128]{1,0:T(1,128)S(1)} %bitcast.1, s32[16]{0:T(128)S(1)} %copy-done.2, bf16[1024,1024]{1,0:T(8,128)(2,1)S(1)} %copy-done.3, bf16[112,1024]{1,0:T(8,128)(2,1)S(1)} %copy-done.4), custom_call_target="tpu_custom_call" | custom-call | flops 3000000000 | bytes 8000000 | tf_op jit(solution)/shard_map/pallas_call | solution.py:371
  47.7 0.7 %copy.6 = f32[4,101,128]{2,0,1:T(4,128)} copy(f32[4,101,128]{2,1,0:T(8,128)S(1)} %shard_map.55) | data formatting | bytes 413696 | tf_op jit(solution)/shard_map/pallas_call | solution.py:371
Async XLA Ops:
  0.0 1.2 %copy-start = (bf16[4,1024,128]{2,1,0:T(8,128)(2,1)S(1)}, bf16[4,1024,128]{2,1,0:T(8,128)(2,1)}, u32[]{:S(2)}) copy-start(bf16[4,1024,128]{2,1,0:T(8,128)(2,1)} %raw.1) | copy-start | bytes 3145732
  1.2 0.7 %copy-start.1 = (s32[128]{0:T(128)S(1)}, s32[128]{0:T(128)}, u32[]{:S(2)}) copy-start(s32[128]{0:T(128)} %param.7) | copy-start | bytes 1540
  1.9 0.7 %copy-start.2 = (s32[16]{0:T(128)S(1)}, s32[16]{0:T(128)}, u32[]{:S(2)}) copy-start(s32[16]{0:T(128)} %cnt.1) | copy-start | bytes 196
  2.5 1.6 %copy-start.3 = (bf16[1024,1024]{1,0:T(8,128)(2,1)S(1)}, bf16[1024,1024]{1,0:T(8,128)(2,1)}, u32[]{:S(2)}) copy-start(bf16[1024,1024]{1,0:T(8,128)(2,1)} %constant.4.clone.basis_hbm) | copy-start | bytes 6291460
  4.1 0.9 %copy-start.4 = (bf16[112,1024]{1,0:T(8,128)(2,1)S(1)}, bf16[112,1024]{1,0:T(8,128)(2,1)}, u32[]{:S(2)}) copy-start(bf16[112,1024]{1,0:T(8,128)(2,1)} %constant.5.clone.inv) | copy-start | bytes 688132

commit v2 on v1

--- a/solution.py
+++ b/solution.py
@@ -42,9 +42,9 @@
 
 def kernel(
     size,
-    raw, mask, cnt, basis_hbm, inv,
+    raw, mask_hbm, cnt_hbm, basis_hbm, inv_hbm,
     out,
-    basis, own_raw, nb_raw, mask_out, mask_in, spec, power, w0, wu, wl, prods, acc,
+    mask, cnt, inv, basis, own_raw, nb_raw, mask_out, mask_in, spec, power, w0, wu, wl, prods, acc,
     home, mid, home_in, mid_in, hsend, msend, hrecv, mrecv,
     load_sem, xs, xr, us, ur, ds, dr, cs, cr, es, er, ms, mr,
 ):
@@ -72,10 +72,17 @@
         for s in range(kept)
     ]
     basis_load = pltpu.make_async_copy(basis_hbm, basis, load_sem.at[kept])
+    mask_load = pltpu.make_async_copy(mask_hbm, mask, load_sem.at[kept + 1])
+    cnt_load = pltpu.make_async_copy(cnt_hbm, cnt, load_sem.at[kept + 2])
+    inv_load = pltpu.make_async_copy(inv_hbm, inv, load_sem.at[kept + 3])
+    mask_load.start()
+    cnt_load.start()
     raw_load[0].start()
     basis_load.start()
     for s in range(1, kept):
         raw_load[s].start()
+    inv_load.start()
+    mask_load.wait()
     mask_out[...] = jnp.broadcast_to(mask[...], mask_out.shape)
 
     barrier = pltpu.get_barrier_semaphore()
@@ -245,6 +252,7 @@
         return jnp.dot(inv[...], prods[i], preferred_element_type=F32)
 
     own_at, nb_at = side, 1 - side
+    cnt_load.wait()
     raw_load[0].wait()
     basis_load.wait()
     whiten(own_raw.at[0], mask[...], cable, 0, w0.at[0, own_at])
@@ -263,6 +271,7 @@
     arrive(0, 0, own_at)
     arrive(1, 0, nb_at)
     crosses(0)
+    inv_load.wait()
     for i in range(9):
         acc[i] = lags(i)
     arrive(2, 1, own_at)
@@ -371,15 +380,12 @@
     return pl.pallas_call(
         functools.partial(kernel, size),
         out_shape=jax.ShapeDtypeStruct((HALF, LAGS, chan), F32),
-        in_specs=[
-            pl.BlockSpec(memory_space=pl.ANY),
-            vmem,
-            pl.BlockSpec(memory_space=pltpu.SMEM),
-            pl.BlockSpec(memory_space=pl.ANY),
-            vmem,
-        ],
+        in_specs=[pl.BlockSpec(memory_space=pltpu.HBM)] * 5,
         out_specs=vmem,
         scratch_shapes=[
+            pltpu.VMEM((1, 128), jnp.int32),
+            pltpu.SMEM(seg_count.shape, jnp.int32),
+            pltpu.VMEM((ROWS, samples), BF16),
             pltpu.VMEM((samples, samples), BF16),
             pltpu.VMEM((kept, samples, 128), BF16),
             pltpu.VMEM((kept, samples, 128), BF16),
@@ -398,7 +404,7 @@
             lagged,
             pltpu.VMEM((HALF, ROWS, 128), BF16),
             lagged,
-            dma((kept + 1,)),
+            dma((kept + 4,)),
             dma((kept + 1,)), dma((kept + 1,)),
             dma((4,)), dma((4,)), dma((4,)), dma((4,)),
             dma((2,)), dma((2,)),

time: 48.6 us -> 48.3 us (level)
  no operation moved by 1% of the time
where the time goes in v2:
time: 48.3 us; the launch traced here: 48.1 us
  Pallas kernels  42.3 us (88%)
  local copies, waits for them, and re-layouts  5.8 us (12%)
    pallas_call x1, Pallas kernels, body(): pl.pallas_call(functools.partial(kernel, size), out_shape=jax.ShapeDtypeS...  42.3 us
    unnamed x10, local copies, waits for them, and re-layouts  5.06 us

profile of v2, /device:TPU:1, one launch (start us, length us, event | category | flops | bytes accessed | tf_op | source)
XLA Modules:
  0.0 48.1 jit_solution(4727882655243998152)
XLA Ops:
  0.0 0.0 copy-start
  0.0 1.2 %copy-done = bf16[4,1024,128]{2,1,0:T(8,128)(2,1)S(1)} copy-done((bf16[4,1024,128]{2,1,0:T(8,128)(2,1)S(1)}, bf16[4,1024,128]{2,1,0:T(8,128)(2,1)}, u32[]{:S(2)}) %copy-start) | copy-done | bytes 1048600
  1.2 0.0 copy-start.1
  1.2 0.7 %copy-done.1 = s32[128]{0:T(128)S(1)} copy-done((s32[128]{0:T(128)S(1)}, s32[128]{0:T(128)}, u32[]{:S(2)}) %copy-start.1) | copy-done | bytes 536
  1.9 0.0 copy-start.2
  1.9 0.7 %copy-done.2 = s32[16]{0:T(128)S(1)} copy-done((s32[16]{0:T(128)S(1)}, s32[16]{0:T(128)}, u32[]{:S(2)}) %copy-start.2) | copy-done | bytes 88
  2.5 0.0 copy-start.3
  2.5 1.6 %copy-done.3 = bf16[1024,1024]{1,0:T(8,128)(2,1)S(1)} copy-done((bf16[1024,1024]{1,0:T(8,128)(2,1)S(1)}, bf16[1024,1024]{1,0:T(8,128)(2,1)}, u32[]{:S(2)}) %copy-start.3) | copy-done | bytes 2097176
  4.1 0.0 copy-start.4
  4.1 0.9 %copy-done.4 = bf16[112,1024]{1,0:T(8,128)(2,1)S(1)} copy-done((bf16[112,1024]{1,0:T(8,128)(2,1)S(1)}, bf16[112,1024]{1,0:T(8,128)(2,1)}, u32[]{:S(2)}) %copy-start.4) | copy-done | bytes 229400
  5.1 42.3 %shard_map.55 = f32[4,101,128]{2,1,0:T(8,128)S(1)} custom-call(bf16[4,1024,128]{2,1,0:T(8,128)(2,1)S(1)} %copy-done, s32[1,128]{1,0:T(1,128)S(1)} %bitcast.1, s32[16]{0:T(128)S(1)} %copy-done.2, bf16[1024,1024]{1,0:T(8,128)(2,1)S(1)} %copy-done.3, bf16[112,1024]{1,0:T(8,128)(2,1)S(1)} %copy-done.4), custom_call_target="tpu_custom_call" | custom-call | flops 3000000000 | bytes 8000000 | tf_op jit(solution)/shard_map/pallas_call | solution.py:380
  47.4 0.7 %copy.6 = f32[4,101,128]{2,0,1:T(4,128)} copy(f32[4,101,128]{2,1,0:T(8,128)S(1)} %shard_map.55) | data formatting | bytes 413696 | tf_op jit(solution)/shard_map/pallas_call | solution.py:380
Async XLA Ops:
  0.0 1.2 %copy-start = (bf16[4,1024,128]{2,1,0:T(8,128)(2,1)S(1)}, bf16[4,1024,128]{2,1,0:T(8,128)(2,1)}, u32[]{:S(2)}) copy-start(bf16[4,1024,128]{2,1,0:T(8,128)(2,1)} %raw.1) | copy-start | bytes 3145732
  1.2 0.7 %copy-start.1 = (s32[128]{0:T(128)S(1)}, s32[128]{0:T(128)}, u32[]{:S(2)}) copy-start(s32[128]{0:T(128)} %param.7) | copy-start | bytes 1540
  1.9 0.7 %copy-start.2 = (s32[16]{0:T(128)S(1)}, s32[16]{0:T(128)}, u32[]{:S(2)}) copy-start(s32[16]{0:T(128)} %cnt_hbm.1) | copy-start | bytes 196
  2.5 1.6 %copy-start.3 = (bf16[1024,1024]{1,0:T(8,128)(2,1)S(1)}, bf16[1024,1024]{1,0:T(8,128)(2,1)}, u32[]{:S(2)}) copy-start(bf16[1024,1024]{1,0:T(8,128)(2,1)} %constant.4.clone.basis_hbm) | copy-start | bytes 6291460
  4.1 0.9 %copy-start.4 = (bf16[112,1024]{1,0:T(8,128)(2,1)S(1)}, bf16[112,1024]{1,0:T(8,128)(2,1)}, u32[]{:S(2)}) copy-start(bf16[112,1024]{1,0:T(8,128)(2,1)} %constant.5.clone.inv_hbm) | copy-start | bytes 688132

commit v3 on v2

--- a/solution.py
+++ b/solution.py
@@ -15,15 +15,21 @@
 ROWS = 112
 NOFF = 8
 HALF = NOFF // 2
+PIECES = 4
 F32 = jnp.float32
 BF16 = jnp.bfloat16
 MESH = pl.DeviceIdType.MESH
 
 
+def row_order(samples):
+    return np.arange(samples).reshape(2, PIECES, -1).transpose(1, 0, 2).reshape(-1)
+
+
 def forward_table(samples):
     bins = samples // 2
     phase = np.outer(np.arange(bins), np.arange(samples)) % samples * (2.0 * math.pi / samples)
-    return np.concatenate([np.cos(phase), -np.sin(phase)], axis=0).astype(ml_dtypes.bfloat16)
+    table = np.concatenate([np.cos(phase), -np.sin(phase)], axis=0)
+    return table[row_order(samples)].astype(ml_dtypes.bfloat16)
 
 
 def lag_table(samples):
@@ -32,7 +38,7 @@
     phase = np.outer(lag, np.arange(bins)) % samples * (2.0 * math.pi / samples)
     table = np.concatenate([np.cos(phase), -np.sin(phase)], axis=1) / math.sqrt(bins)
     full = np.zeros((ROWS, samples), np.float64)
-    full[:LAGS] = table
+    full[:LAGS] = table[:, row_order(samples)]
     return full.astype(ml_dtypes.bfloat16)
 
 
@@ -60,6 +66,13 @@
     nblk = cnt.shape[0]
     seg_dev = raw.shape[0]
     kept = seg_dev // 2
+    part = samples // PIECES
+    part_bins = part // 2
+
+    def rows_of(t, tile):
+        per = part_bins // tile
+        re = pl.multiple_of(t // per * part + t % per * tile, tile)
+        return pl.ds(re, tile), pl.ds(pl.multiple_of(re + part_bins, tile), tile)
 
     def remote(src, dst, ssem, rsem, at, core):
         return pltpu.make_async_remote_copy(
@@ -121,8 +134,6 @@
     home[1, 0, 3] = zero_tile
     for kk in range(1, 4):
         home[1, 1, kk] = zero_tile
-    mid[0, 0] = zero_tile
-    mid[0, 1] = zero_tile
 
     @pl.when(jnp.logical_not(has_up))
     def _():
@@ -166,8 +177,9 @@
 
         def powers(t, total):
             at = pl.multiple_of(t * 64, 64)
-            re = spec[pl.ds(at, 64), :]
-            im = spec[pl.ds(bins + at, 64), :]
+            re_at, im_at = rows_of(t, 64)
+            re = spec[re_at, :]
+            im = spec[im_at, :]
             p = re * re + im * im
             power[pl.ds(8 + at, 64), :] = p
             return total + jnp.sum(p.reshape(8, 8, 128), axis=0)
@@ -181,16 +193,22 @@
             wide = power[pl.ds(at, 80), :]
             smooth = wide[6:70] + wide[7:71] + wide[8:72] + wide[9:73] + wide[10:74]
             factor = keep * lax.rsqrt(smooth * 0.2 + floor)
-            dst[pl.ds(at, 64), :] = (spec[pl.ds(at, 64), :] * factor).astype(BF16)
-            dst[pl.ds(bins + at, 64), :] = (spec[pl.ds(bins + at, 64), :] * factor).astype(BF16)
-
-    def chunk_copies(q, s, col):
-        up = remote(w0.at[s, col], wl.at[s, col], us.at[q], dr.at[q], cable + 2, fold)
-        dn = remote(w0.at[s, col], wu.at[s, col], ds.at[q], ur.at[q], cable - 2, fold)
+            for rows in rows_of(t, 64):
+                dst[rows, :] = (spec[rows, :] * factor).astype(BF16)
+
+    own_at, nb_at = side, 1 - side
+    whole = pl.ds(0, samples)
+    chunks = [(0, own_at, whole), (0, nb_at, whole), (1, own_at, whole)]
+    chunks += [(1, nb_at, pl.ds(p * part, part)) for p in range(PIECES)]
+
+    def chunk_copies(q):
+        at = chunks[q]
+        up = remote(w0.at[at], wl.at[at], us.at[q], dr.at[q], cable + 2, fold)
+        dn = remote(w0.at[at], wu.at[at], ds.at[q], ur.at[q], cable - 2, fold)
         return up, dn
 
-    def send(q, s, col):
-        up, dn = chunk_copies(q, s, col)
+    def send(q):
+        up, dn = chunk_copies(q)
 
         @pl.when(has_up)
         def _():
@@ -200,8 +218,8 @@
         def _():
             dn.start()
 
-    def arrive(q, s, col):
-        up, dn = chunk_copies(q, s, col)
+    def arrive(q):
+        up, dn = chunk_copies(q)
 
         @pl.when(has_dn)
         def _():
@@ -211,15 +229,15 @@
         def _():
             dn.wait_recv()
 
-    def crosses(s):
-        @pl.loop(0, bins // 16)
+    def crosses(s, first, last):
+        @pl.loop(first * (part_bins // 16), last * (part_bins // 16))
         def _(t):
-            at = pl.multiple_of(t * 16, 16)
+            re_at, im_at = rows_of(t, 16)
 
             def load(ref, col):
                 return (
-                    ref[s, col, pl.ds(at, 16), :].astype(F32),
-                    ref[s, col, pl.ds(bins + at, 16), :].astype(F32),
+                    ref[s, col, re_at, :].astype(F32),
+                    ref[s, col, im_at, :].astype(F32),
                 )
 
             e0, e1 = load(w0, 0), load(w0, 1)
@@ -238,116 +256,143 @@
             jobs += [((e0, e1)[key[0]], ext[key]) for key in HOME]
             for i, (a, b) in enumerate(jobs):
                 lanes = slice(i % 2 * 128, i % 2 * 128 + 128)
-                prods[i // 2, pl.ds(at, 16), lanes] = (a[0] * b[0] + a[1] * b[1]).astype(BF16)
-                prods[i // 2, pl.ds(bins + at, 16), lanes] = (a[1] * b[0] - a[0] * b[1]).astype(BF16)
+                prods[i // 2, re_at, lanes] = (a[0] * b[0] + a[1] * b[1]).astype(BF16)
+                prods[i // 2, im_at, lanes] = (a[1] * b[0] - a[0] * b[1]).astype(BF16)
 
     def slot(i):
         if i < len(MID):
-            col, k = MID[i]
-            return mid.at[col, k - 1 - HALF]
+            return mid.at[i]
         col, k = HOME[i - len(MID)]
         return home.at[(k - 1) // HALF, col, (k - 1) % HALF]
 
-    def lags(i):
-        return jnp.dot(inv[...], prods[i], preferred_element_type=F32)
-
-    own_at, nb_at = side, 1 - side
+    def lags(i, rows):
+        return jnp.dot(inv[:, rows], prods[i, rows, :], preferred_element_type=F32)
+
     cnt_load.wait()
     raw_load[0].wait()
     basis_load.wait()
     whiten(own_raw.at[0], mask[...], cable, 0, w0.at[0, own_at])
-    send(0, 0, own_at)
+    send(0)
     raw_load[1].wait()
     whiten(own_raw.at[1], mask[...], cable, 1, w0.at[1, own_at])
     x_mask.wait_recv()
     x_raw[0].wait_recv()
     whiten(nb_raw.at[0], mask_in[0:1, :], peer, 0, w0.at[0, nb_at])
-    send(1, 0, nb_at)
-    send(2, 1, own_at)
+    send(1)
+    send(2)
     x_raw[1].wait_recv()
     whiten(nb_raw.at[1], mask_in[0:1, :], peer, 1, w0.at[1, nb_at])
-    send(3, 1, nb_at)
-
-    arrive(0, 0, own_at)
-    arrive(1, 0, nb_at)
-    crosses(0)
+    for p in range(PIECES):
+        send(3 + p)
+
+    arrive(0)
+    arrive(1)
+    crosses(0, 0, PIECES)
     inv_load.wait()
     for i in range(9):
-        acc[i] = lags(i)
-    arrive(2, 1, own_at)
-    arrive(3, 1, nb_at)
-    crosses(1)
-
-    def finish(i):
-        total = acc[i] + lags(i)
-        slot(2 * i)[...] = total[:, :128].astype(BF16)
-        slot(2 * i + 1)[...] = total[:, 128:].astype(BF16)
-
-    for i in range(3):
-        finish(i)
+        acc[i] = lags(i, slice(0, samples))
+    arrive(2)
+
     c_mid = remote(mid, mid_in, cs.at[0], cr.at[0], cable, 1 - fold)
-
-    @pl.when(fold == 0)
-    def _():
-        c_mid.start()
-
-    for i in range(3, 9):
-        finish(i)
+    for p in range(PIECES):
+        arrive(3 + p)
+        crosses(1, p, p + 1)
+        for i in range(9):
+            total = acc[i] + lags(i, slice(p * part, (p + 1) * part))
+            if p < PIECES - 1:
+                acc[i] = total
+                continue
+            slot(2 * i)[...] = total[:, :128].astype(BF16)
+            slot(2 * i + 1)[...] = total[:, 128:].astype(BF16)
+            if 2 * i + 2 == len(MID):
+
+                @pl.when(fold == 0)
+                def _():
+                    c_mid.start()
+
     c_home = remote(home.at[1 - fold], home_in, cs.at[1], cr.at[1], cable, 1 - fold)
     c_home.start()
 
-    m_near = remote(msend.at[side], mrecv.at[0], ms.at[0], mr.at[0], cable - 2, fold)
-    m_diag = remote(msend.at[1 - side], mrecv.at[1], ms.at[1], mr.at[1], peer - 2, fold)
+    def mid_copies():
+        for at in range(2):
+            tiles = (pl.ds(0, 2), pl.ds(2, 4))
+            there = (pl.ds(0, 2), pl.ds(0, 4))
+            near = remote(msend.at[tiles[at]], mrecv.at[0, there[at]], ms.at[0], mr.at[0], cable - 2, fold)
+            diag = remote(msend.at[tiles[1 - at]], mrecv.at[1, there[1 - at]], ms.at[1], mr.at[1], peer - 2, fold)
+            yield side == at, near, diag
+
+    def home_copies():
+        yield fold == 0, HALF, remote(hsend, hrecv, es.at[0], er.at[0], peer, fold)
+        for at, tiles in ((0, 1), (1, 3)):
+            some = pl.ds(0, tiles)
+            on = jnp.logical_and(fold == 1, side == at)
+            yield on, tiles, remote(hsend.at[some], hrecv.at[some], es.at[0], er.at[0], peer, fold)
+
+    sends_mid = jnp.logical_and(fold == 1, has_dn)
+    gets_mid = jnp.logical_and(fold == 1, has_up)
 
     @pl.when(fold == 1)
     def _():
         c_mid.wait_recv()
-        for col in range(2):
-            for kk in range(HALF):
-                msend[col, kk] = (mid[col, kk].astype(F32) + mid_in[col, kk].astype(F32)).astype(BF16)
-
-        @pl.when(has_dn)
-        def _():
-            m_near.start()
-            m_diag.start()
+        for i in range(len(MID)):
+            msend[i] = (mid[i].astype(F32) + mid_in[i].astype(F32)).astype(BF16)
+
+    for on, near, diag in mid_copies():
+
+        @pl.when(jnp.logical_and(sends_mid, on))
+        def _():
+            diag.start()
+            near.start()
 
     c_home.wait_recv()
+    for on, tiles, copy in home_copies():
+
+        @pl.when(on)
+        def _():
+            for kk in range(tiles):
+                hsend[kk] = (
+                    home[fold, 1 - side, kk].astype(F32) + home_in[1 - side, kk].astype(F32)
+                ).astype(BF16)
+            copy.start()
+
     for kk in range(HALF):
-        hsend[kk] = (
-            home[fold, 1 - side, kk].astype(F32) + home_in[1 - side, kk].astype(F32)
-        ).astype(BF16)
-    e_home = remote(hsend, hrecv, es.at[0], er.at[0], peer, fold)
-    e_home.start()
-    for kk in range(HALF):
-        acc[0, :, 0:128] = home[fold, side, kk].astype(F32) + home_in[side, kk].astype(F32)
-        out[kk] = acc[0, 0:LAGS, 0:128]
-    e_home.wait_recv()
+        acc[kk, :, 0:128] = home[fold, side, kk].astype(F32) + home_in[side, kk].astype(F32)
+
+    e_side = [(fold == 0, HALF, hrecv)]
+    e_side += [(jnp.logical_and(fold == 1, side == at), tiles, hrecv) for at, tiles in ((0, 3), (1, 1))]
+    for on, tiles, ref in e_side:
+
+        @pl.when(on)
+        def _():
+            some = ref.at[pl.ds(0, tiles)]
+            remote(some, some, es.at[0], er.at[0], peer, fold).wait_recv()
+            for kk in range(tiles):
+                acc[kk, :, 0:128] += ref[kk].astype(F32)
+
+    for at, tiles in ((0, 2), (1, 4)):
+
+        @pl.when(jnp.logical_and(gets_mid, side == at))
+        def _():
+            for j in range(2):
+                some = mrecv.at[j, pl.ds(0, tiles)]
+                remote(some, some, ms.at[j], mr.at[j], peer, fold).wait_recv()
+            for i in range(tiles):
+                acc[HALF - tiles + i, :, 0:128] += mrecv[0, i].astype(F32) + mrecv[1, i].astype(F32)
 
     def count_of(block):
         return jnp.where(block < nblk, cnt[jnp.minimum(block, nblk - 1)], 0)
-
-    with_mid = jnp.logical_and(fold == 1, has_up)
-
-    @pl.when(with_mid)
-    def _():
-        m_near.wait_recv()
-        m_diag.wait_recv()
-        for kk in range(HALF):
-            acc[0, :, 0:128] = mrecv[0, kk].astype(F32) + mrecv[1, kk].astype(F32)
-            out[kk] += acc[0, 0:LAGS, 0:128]
 
     for kk in range(HALF):
         k = fold * HALF + kk + 1
         pair = [jnp.minimum(cnt[2 * cable + b], count_of(2 * cable + b + k)) for b in range(2)]
         divisor = jnp.maximum(jnp.where(low, pair[0], pair[1]), 1).astype(F32)
-        acc[0, :, 0:128] = hrecv[kk].astype(F32)
-        out[kk] = (out[kk] + acc[0, 0:LAGS, 0:128]) / divisor
+        out[pl.ds(kk, LAGS, stride=HALF), :] = acc[kk, 0:LAGS, 0:128] / divisor
 
     x_mask.wait_send()
     for copy in x_raw:
         copy.wait_send()
-    for q, (s, col) in enumerate([(0, own_at), (0, nb_at), (1, own_at), (1, nb_at)]):
-        up, dn = chunk_copies(q, s, col)
+    for q in range(len(chunks)):
+        up, dn = chunk_copies(q)
 
         @pl.when(has_up)
         def _():
@@ -362,12 +407,18 @@
         c_mid.wait_send()
 
     c_home.wait_send()
-    e_home.wait_send()
-
-    @pl.when(jnp.logical_and(fold == 1, has_dn))
-    def _():
-        m_near.wait_send()
-        m_diag.wait_send()
+    for on, tiles, copy in home_copies():
+
+        @pl.when(on)
+        def _():
+            copy.wait_send()
+
+    for on, near, diag in mid_copies():
+
+        @pl.when(jnp.logical_and(sends_mid, on))
+        def _():
+            near.wait_send()
+            diag.wait_send()
 
 
 def body(size, raw, seg_count, mask):
@@ -377,9 +428,10 @@
     dma = pltpu.SemaphoreType.DMA
     white = pltpu.VMEM((kept, 2, samples, 128), BF16)
     lagged = pltpu.VMEM((2, HALF, ROWS, 128), BF16)
-    return pl.pallas_call(
+    mids = pltpu.VMEM((len(MID), ROWS, 128), BF16)
+    lagged_sums = pl.pallas_call(
         functools.partial(kernel, size),
-        out_shape=jax.ShapeDtypeStruct((HALF, LAGS, chan), F32),
+        out_shape=jax.ShapeDtypeStruct((LAGS * HALF, chan), F32),
         in_specs=[pl.BlockSpec(memory_space=pltpu.HBM)] * 5,
         out_specs=vmem,
         scratch_shapes=[
@@ -397,25 +449,26 @@
             pltpu.VMEM((9, samples, 256), BF16),
             pltpu.VMEM((9, ROWS, 256), F32),
             pltpu.VMEM((2, 2, HALF, ROWS, 128), BF16),
+            mids,
             lagged,
-            lagged,
-            lagged,
+            mids,
             pltpu.VMEM((HALF, ROWS, 128), BF16),
-            lagged,
+            mids,
             pltpu.VMEM((HALF, ROWS, 128), BF16),
             lagged,
             dma((kept + 4,)),
             dma((kept + 1,)), dma((kept + 1,)),
-            dma((4,)), dma((4,)), dma((4,)), dma((4,)),
+            dma((3 + PIECES,)), dma((3 + PIECES,)), dma((3 + PIECES,)), dma((3 + PIECES,)),
             dma((2,)), dma((2,)),
             dma((1,)), dma((1,)),
             dma((2,)), dma((2,)),
         ],
         compiler_params=pltpu.CompilerParams(
-            collective_id=0, has_side_effects=True, vmem_limit_bytes=40 * 1024 * 1024
+            collective_id=0, has_side_effects=True, vmem_limit_bytes=63 * 1024 * 1024
         ),
         cost_estimate=pl.CostEstimate(flops=3 * 10**9, bytes_accessed=8 * 10**6, transcendentals=0),
     )(raw, mask.reshape(1, chan), seg_count, jnp.asarray(forward_table(samples)), jnp.asarray(lag_table(samples)))
+    return lagged_sums.reshape(LAGS, HALF, chan).transpose(1, 0, 2)
 
 
 def solution(mesh):

time: 48.3 us -> 42.8 us (0.89)
  local copies, waits for them, and re-layouts: 5.8 us -> 1.67 us
  Pallas kernels: 42.3 us -> 40.8 us
    unnamed x10 -> x0, local copies, waits for them, and re-layouts: 5.06 us -> none
    reshape x0 -> x1, local copies, waits for them, and re-layouts: none -> 1.67 us  [body(): return lagged_sums.reshape(LAGS, HALF, chan).transpose(1, 0, 2)]
    pallas_call x1, Pallas kernels: 42.3 us -> 40.8 us  [body(): pl.pallas_call(functools.partial(kernel, size), out_shape=jax.ShapeDtypeS...]
    pallas_call x1 -> x0, local copies, waits for them, and re-layouts: 0.73 us -> none  [body(): pl.pallas_call(functools.partial(kernel, size), out_shape=jax.ShapeDtypeS...]
where the time goes in v3:
time: 42.8 us; the launch traced here: 42.4 us
  Pallas kernels  40.8 us (95%)
  local copies, waits for them, and re-layouts  1.67 us (4%)
    pallas_call x1, Pallas kernels, body(): pl.pallas_call(functools.partial(kernel, size), out_shape=jax.ShapeDtypeS...  40.8 us
    reshape x1, local copies, waits for them, and re-layouts, body(): return lagged_sums.reshape(LAGS, HALF, chan).transpose(1, 0, 2)  1.67 us

profile of v3, /device:TPU:1, one launch (start us, length us, event | category | flops | bytes accessed | tf_op | source)
XLA Modules:
  0.0 42.4 jit_solution(9492203168575576057)
XLA Ops:
  0.0 40.8 %shard_map.55 = f32[404,128]{1,0:T(8,128)} custom-call(bf16[4,1024,128]{2,1,0:T(8,128)(2,1)} %raw.1, s32[1,128]{1,0:T(1,128)} %bitcast.2, s32[16]{0:T(128)} %cnt_hbm.1, bf16[1024,1024]{1,0:T(8,128)(2,1)} %constant.4.clone.basis_hbm, bf16[112,1024]{1,0:T(8,128)(2,1)} %constant.5.clone.inv_hbm), custom_call_target="tpu_custom_call" | custom-call | flops 3000000000 | bytes 8000000 | tf_op jit(solution)/shard_map/pallas_call | solution.py:432
  40.8 1.7 %reshape.7 = f32[101,4,128]{2,1,0:T(4,128)} reshape(f32[404,128]{1,0:T(8,128)} %shard_map.55) | data formatting | bytes 413696 | tf_op jit(solution)/shard_map/reshape | solution.py:471

commit v4 on v3

--- a/solution.py
+++ b/solution.py
@@ -80,6 +80,24 @@
             device_id={"cable": at, "fold": core}, device_id_type=MESH,
         )
 
+    barrier = pltpu.get_barrier_semaphore()
+
+    def greet(at, core):
+        pl.semaphore_signal(barrier, inc=1, device_id={"cable": at, "fold": core}, device_id_type=MESH)
+
+    greet(peer, fold)
+    greet(cable, 1 - fold)
+
+    @pl.when(has_up)
+    def _():
+        greet(cable + 2, fold)
+        greet(peer + 2, fold)
+
+    @pl.when(has_dn)
+    def _():
+        greet(cable - 2, fold)
+        greet(peer - 2, fold)
+
     raw_load = [
         pltpu.make_async_copy(raw.at[kept * side + s], own_raw.at[s], load_sem.at[s])
         for s in range(kept)
@@ -97,36 +115,6 @@
     inv_load.start()
     mask_load.wait()
     mask_out[...] = jnp.broadcast_to(mask[...], mask_out.shape)
-
-    barrier = pltpu.get_barrier_semaphore()
-
-    def greet(at, core):
-        pl.semaphore_signal(barrier, inc=1, device_id={"cable": at, "fold": core}, device_id_type=MESH)
-
-    greet(peer, fold)
-    greet(cable, 1 - fold)
-
-    @pl.when(has_up)
-    def _():
-        greet(cable + 2, fold)
-        greet(peer + 2, fold)
-
-    @pl.when(has_dn)
-    def _():
-        greet(cable - 2, fold)
-        greet(peer - 2, fold)
-
-    peers = 2 + jnp.where(has_up, 2, 0) + jnp.where(has_dn, 2, 0)
-    pl.semaphore_wait(barrier, peers)
-
-    x_raw = [
-        remote(raw.at[kept * (1 - side) + s], nb_raw.at[s], xs.at[s], xr.at[s], peer, fold)
-        for s in range(kept)
-    ]
-    x_mask = remote(mask_out, mask_in, xs.at[kept], xr.at[kept], peer, fold)
-    x_mask.start()
-    for copy in x_raw:
-        copy.start()
 
     power[0:8, :] = jnp.zeros((8, 128), F32)
     power[bins + 8 : bins + 16, :] = jnp.zeros((8, 128), F32)
@@ -272,6 +260,16 @@
     raw_load[0].wait()
     basis_load.wait()
     whiten(own_raw.at[0], mask[...], cable, 0, w0.at[0, own_at])
+    peers = 2 + jnp.where(has_up, 2, 0) + jnp.where(has_dn, 2, 0)
+    pl.semaphore_wait(barrier, peers)
+    x_raw = [
+        remote(raw.at[kept * (1 - side) + s], nb_raw.at[s], xs.at[s], xr.at[s], peer, fold)
+        for s in range(kept)
+    ]
+    x_mask = remote(mask_out, mask_in, xs.at[kept], xr.at[kept], peer, fold)
+    x_mask.start()
+    for copy in x_raw:
+        copy.start()
     send(0)
     raw_load[1].wait()
     whiten(own_raw.at[1], mask[...], cable, 1, w0.at[1, own_at])
@@ -386,7 +384,7 @@
         k = fold * HALF + kk + 1
         pair = [jnp.minimum(cnt[2 * cable + b], count_of(2 * cable + b + k)) for b in range(2)]
         divisor = jnp.maximum(jnp.where(low, pair[0], pair[1]), 1).astype(F32)
-        out[pl.ds(kk, LAGS, stride=HALF), :] = acc[kk, 0:LAGS, 0:128] / divisor
+        out[kk] = acc[kk, 0:LAGS, 0:128] / divisor
 
     x_mask.wait_send()
     for copy in x_raw:
@@ -431,7 +429,7 @@
     mids = pltpu.VMEM((len(MID), ROWS, 128), BF16)
     lagged_sums = pl.pallas_call(
         functools.partial(kernel, size),
-        out_shape=jax.ShapeDtypeStruct((LAGS * HALF, chan), F32),
+        out_shape=jax.ShapeDtypeStruct((HALF, LAGS, chan), F32),
         in_specs=[pl.BlockSpec(memory_space=pltpu.HBM)] * 5,
         out_specs=vmem,
         scratch_shapes=[
@@ -468,7 +466,7 @@
         ),
         cost_estimate=pl.CostEstimate(flops=3 * 10**9, bytes_accessed=8 * 10**6, transcendentals=0),
     )(raw, mask.reshape(1, chan), seg_count, jnp.asarray(forward_table(samples)), jnp.asarray(lag_table(samples)))
-    return lagged_sums.reshape(LAGS, HALF, chan).transpose(1, 0, 2)
+    return lagged_sums
 
 
 def solution(mesh):

time: 42.8 us -> 44.2 us (1.033)
  Pallas kernels: 40.8 us -> 42.4 us
    reshape x1 -> x0, local copies, waits for them, and re-layouts: 1.67 us -> none  [body(): return lagged_sums.reshape(LAGS, HALF, chan).transpose(1, 0, 2)]
    pallas_call x0 -> x1, local copies, waits for them, and re-layouts: none -> 1.67 us  [body(): pl.pallas_call(functools.partial(kernel, size), out_shape=jax.ShapeDtypeS...]
    pallas_call x1, Pallas kernels: 40.8 us -> 42.4 us  [body(): pl.pallas_call(functools.partial(kernel, size), out_shape=jax.ShapeDtypeS...]
where the time goes in v4:
time: 44.2 us; the launch traced here: 44.1 us
  Pallas kernels  42.4 us (96%)
  local copies, waits for them, and re-layouts  1.67 us (4%)
    pallas_call x1, Pallas kernels, body(): pl.pallas_call(functools.partial(kernel, size), out_shape=jax.ShapeDtypeS...  42.4 us
    pallas_call x1, local copies, waits for them, and re-layouts, body(): pl.pallas_call(functools.partial(kernel, size), out_shape=jax.ShapeDtypeS...  1.67 us

profile of v4, /device:TPU:1, one launch (start us, length us, event | category | flops | bytes accessed | tf_op | source)
XLA Modules:
  0.0 44.1 jit_solution(1469753434664596531)
XLA Ops:
  0.0 42.4 %shard_map.55 = f32[4,101,128]{2,1,0:T(8,128)} custom-call(bf16[4,1024,128]{2,1,0:T(8,128)(2,1)} %raw.1, s32[1,128]{1,0:T(1,128)} %bitcast.1, s32[16]{0:T(128)} %cnt_hbm.1, bf16[1024,1024]{1,0:T(8,128)(2,1)} %constant.4.clone.basis_hbm, bf16[112,1024]{1,0:T(8,128)(2,1)} %constant.5.clone.inv_hbm), custom_call_target="tpu_custom_call" | custom-call | flops 3000000000 | bytes 8000000 | tf_op jit(solution)/shard_map/pallas_call | solution.py:430
  42.4 1.7 %copy.6 = f32[4,101,128]{2,0,1:T(4,128)} copy(f32[4,101,128]{2,1,0:T(8,128)} %shard_map.55) | data formatting | bytes 413696 | tf_op jit(solution)/shard_map/pallas_call | solution.py:430

commit v5 on v4

--- a/solution.py
+++ b/solution.py
@@ -116,6 +116,18 @@
     mask_load.wait()
     mask_out[...] = jnp.broadcast_to(mask[...], mask_out.shape)
 
+    peers = 2 + jnp.where(has_up, 2, 0) + jnp.where(has_dn, 2, 0)
+    pl.semaphore_wait(barrier, peers)
+
+    x_raw = [
+        remote(raw.at[kept * (1 - side) + s], nb_raw.at[s], xs.at[s], xr.at[s], peer, fold)
+        for s in range(kept)
+    ]
+    x_mask = remote(mask_out, mask_in, xs.at[kept], xr.at[kept], peer, fold)
+    x_mask.start()
+    for copy in x_raw:
+        copy.start()
+
     power[0:8, :] = jnp.zeros((8, 128), F32)
     power[bins + 8 : bins + 16, :] = jnp.zeros((8, 128), F32)
     zero_tile = jnp.zeros((ROWS, 128), BF16)
@@ -260,16 +272,6 @@
     raw_load[0].wait()
     basis_load.wait()
     whiten(own_raw.at[0], mask[...], cable, 0, w0.at[0, own_at])
-    peers = 2 + jnp.where(has_up, 2, 0) + jnp.where(has_dn, 2, 0)
-    pl.semaphore_wait(barrier, peers)
-    x_raw = [
-        remote(raw.at[kept * (1 - side) + s], nb_raw.at[s], xs.at[s], xr.at[s], peer, fold)
-        for s in range(kept)
-    ]
-    x_mask = remote(mask_out, mask_in, xs.at[kept], xr.at[kept], peer, fold)
-    x_mask.start()
-    for copy in x_raw:
-        copy.start()
     send(0)
     raw_load[1].wait()
     whiten(own_raw.at[1], mask[...], cable, 1, w0.at[1, own_at])

time: 44.2 us -> 42.1 us (0.952)
  Pallas kernels: 42.4 us -> 40.1 us
    pallas_call x1, Pallas kernels: 42.4 us -> 40.1 us  [body(): pl.pallas_call(functools.partial(kernel, size), out_shape=jax.ShapeDtypeS...]
where the time goes in v5:
time: 42.1 us; the launch traced here: 41.8 us
  Pallas kernels  40.1 us (95%)
  local copies, waits for them, and re-layouts  1.67 us (4%)
    pallas_call x1, Pallas kernels, body(): pl.pallas_call(functools.partial(kernel, size), out_shape=jax.ShapeDtypeS...  40.1 us
    pallas_call x1, local copies, waits for them, and re-layouts, body(): pl.pallas_call(functools.partial(kernel, size), out_shape=jax.ShapeDtypeS...  1.67 us

profile of v5, /device:TPU:1, one launch (start us, length us, event | category | flops | bytes accessed | tf_op | source)
XLA Modules:
  0.0 41.8 jit_solution(14983977635509442803)
XLA Ops:
  0.0 40.1 %shard_map.55 = f32[4,101,128]{2,1,0:T(8,128)} custom-call(bf16[4,1024,128]{2,1,0:T(8,128)(2,1)} %raw.1, s32[1,128]{1,0:T(1,128)} %bitcast.1, s32[16]{0:T(128)} %cnt_hbm.1, bf16[1024,1024]{1,0:T(8,128)(2,1)} %constant.4.clone.basis_hbm, bf16[112,1024]{1,0:T(8,128)(2,1)} %constant.5.clone.inv_hbm), custom_call_target="tpu_custom_call" | custom-call | flops 3000000000 | bytes 8000000 | tf_op jit(solution)/shard_map/pallas_call | solution.py:432
  40.1 1.7 %copy.6 = f32[4,101,128]{2,0,1:T(4,128)} copy(f32[4,101,128]{2,1,0:T(8,128)} %shard_map.55) | data formatting | bytes 413696 | tf_op jit(solution)/shard_map/pallas_call | solution.py:432

commit v6 on v5

--- a/solution.py
+++ b/solution.py
@@ -275,11 +275,11 @@
     send(0)
     raw_load[1].wait()
     whiten(own_raw.at[1], mask[...], cable, 1, w0.at[1, own_at])
+    send(2)
     x_mask.wait_recv()
     x_raw[0].wait_recv()
     whiten(nb_raw.at[0], mask_in[0:1, :], peer, 0, w0.at[0, nb_at])
     send(1)
-    send(2)
     x_raw[1].wait_recv()
     whiten(nb_raw.at[1], mask_in[0:1, :], peer, 1, w0.at[1, nb_at])
     for p in range(PIECES):

time: 42.1 us -> 43 us (1.021)
  Pallas kernels: 40.1 us -> 41.1 us
    pallas_call x1, Pallas kernels: 40.1 us -> 41.1 us  [body(): pl.pallas_call(functools.partial(kernel, size), out_shape=jax.ShapeDtypeS...]
where the time goes in v6:
time: 43 us; the launch traced here: 42.8 us
  Pallas kernels  41.1 us (96%)
  local copies, waits for them, and re-layouts  1.67 us (4%)
    pallas_call x1, Pallas kernels, body(): pl.pallas_call(functools.partial(kernel, size), out_shape=jax.ShapeDtypeS...  41.1 us
    pallas_call x1, local copies, waits for them, and re-layouts, body(): pl.pallas_call(functools.partial(kernel, size), out_shape=jax.ShapeDtypeS...  1.67 us

profile of v6, /device:TPU:1, one launch (start us, length us, event | category | flops | bytes accessed | tf_op | source)
XLA Modules:
  0.0 42.8 jit_solution(5497773338440159269)
XLA Ops:
  0.0 41.1 %shard_map.55 = f32[4,101,128]{2,1,0:T(8,128)} custom-call(bf16[4,1024,128]{2,1,0:T(8,128)(2,1)} %raw.1, s32[1,128]{1,0:T(1,128)} %bitcast.1, s32[16]{0:T(128)} %cnt_hbm.1, bf16[1024,1024]{1,0:T(8,128)(2,1)} %constant.4.clone.basis_hbm, bf16[112,1024]{1,0:T(8,128)(2,1)} %constant.5.clone.inv_hbm), custom_call_target="tpu_custom_call" | custom-call | flops 3000000000 | bytes 8000000 | tf_op jit(solution)/shard_map/pallas_call | solution.py:432
  41.2 1.7 %copy.6 = f32[4,101,128]{2,0,1:T(4,128)} copy(f32[4,101,128]{2,1,0:T(8,128)} %shard_map.55) | data formatting | bytes 413696 | tf_op jit(solution)/shard_map/pallas_call | solution.py:432
